TPU v7x, 128 devices: a whole 4x4x4 slice. The times are simulated.
128 devices in a mesh: mom: 8 (over y, core), pair: 16 (over x, z).
Axes of the slice: x: 4, y: 4, z: 4, core: 2. Of those that a mesh axis runs over, the one named last changes fastest.
Arguments:
- blocks: bfloat16 [8, 16, 1024, 1024], P('mom', None, 'pair'), may hold values from -1.078125 to 1.078125
- left_ids: int32 [8, 48], P('mom', 'pair'), may hold values from 0 to 15
- right_ids: int32 [8, 48], P('mom', 'pair'), may hold values from 0 to 15
- slice_ids: int32 [8, 48], P('mom', 'pair'), may hold values from 0 to 1
- weight_ids: int32 [8, 48], P('mom', 'pair'), may hold values from 0 to 7
- counts: int32 [8, 16], P('mom', 'pair'), may hold values from 1 to 3, 32 in all within a row
- subduction: float32 [8], replicated, may hold values from -1 to 1
Outputs:
- operator: float32 [8, 1024, 2, 1024], P('mom', 'pair')
Inputs may be any that keep to these rules, and one draw needn't show every extreme that they name: Each row of counts sums to exactly 32.
All inputs are finite; a program needn't handle non-finite values. No bound on the sum of `counts` on one device may be relied on, other than what follows from the above.
Results may differ from a plain program's by a relative error of at most 0.0029.
Values may be sent and summed in bfloat16 or wider, within the bound.
A program may use at most 128 MiB of HBM per device.

v0:
```python
import jax
import jax.numpy as jnp
from jax import lax
from jax.sharding import PartitionSpec as P

PAIR_DEV = 3
SLICES = 2


def partner_2(shard, axis, apart):
    return lax.ppermute(shard, axis, [(i, i ^ 1 << apart) for i in range(lax.axis_size(axis))])


def mixing_table(lefts, rights, slices, weights, allowed, subduction, families):
    total_slots = lefts.shape[0]
    slot = jnp.arange(total_slots, dtype=jnp.int32)
    list_of = slot // PAIR_DEV
    lists = jnp.arange(allowed.shape[0], dtype=jnp.int32)
    limit = jnp.sum(jnp.where(list_of[:, None] == lists[None, :], allowed[None, :], 0), axis=1)
    live = slot % PAIR_DEV < limit
    table_ids = jnp.arange(subduction.shape[0], dtype=jnp.int32)
    looked = jnp.sum(
        jnp.where(weights[:, None] == table_ids[None, :], subduction[None, :], 0.0), axis=1
    )
    select = (slices[:, None] == jnp.arange(SLICES, dtype=jnp.int32)[None, :]).astype(jnp.float32)
    scales = jnp.where(live, looked, 0.0)[:, None] * select
    fam_ids = jnp.arange(families, dtype=jnp.int32)
    right_hot = (rights[:, None] == fam_ids[None, :]).astype(jnp.float32)
    left_hot = (lefts[:, None] == fam_ids[None, :]).astype(jnp.float32)
    return jnp.einsum("kt,kb,ka->tba", scales, right_hot, left_hot, precision=lax.Precision.HIGHEST)


def combine_left(mixing, panels):
    families = panels.shape[0]
    flat = panels.astype(jnp.float32).reshape(families, -1)
    mixed = jnp.dot(
        mixing.reshape(SLICES * families, families), flat, precision=lax.Precision.HIGHEST
    )
    return mixed.astype(jnp.bfloat16).reshape((SLICES, families) + panels.shape[1:])


def body(blocks, left_ids, right_ids, slice_ids, weight_ids, counts, subduction):
    gathered = (
        lax.all_gather(left_ids, "pair", axis=1, tiled=True),
        lax.all_gather(right_ids, "pair", axis=1, tiled=True),
        lax.all_gather(slice_ids, "pair", axis=1, tiled=True),
        lax.all_gather(weight_ids, "pair", axis=1, tiled=True),
        lax.all_gather(counts, "pair", axis=1, tiled=True),
    )
    own = blocks[0]
    families = own.shape[0]
    mixing = mixing_table(
        gathered[0][0],
        gathered[1][0],
        gathered[2][0],
        gathered[3][0],
        gathered[4][0],
        subduction,
        families,
    )
    partner = partner_2(own, "mom", 0)
    combined = combine_left(mixing, own)
    result = jnp.einsum(
        "tbij,bjl->itl",
        combined,
        lax.all_gather(partner, "pair", axis=1, tiled=True),
        preferred_element_type=jnp.float32,
    )
    return result.reshape((1,) + result.shape)


def solution(mesh):
    return jax.shard_map(
        body,
        mesh=mesh,
        in_specs=(
            P("mom", None, "pair", None),
            P("mom", "pair"),
            P("mom", "pair"),
            P("mom", "pair"),
            P("mom", "pair"),
            P("mom", "pair"),
            P(),
        ),
        out_specs=P("mom", "pair", None, None),
        check_vma=False,
    )
```

profile of v0, /device:TPU:1, one launch (start us, length us, event | category | flops | bytes accessed | tf_op | source)
XLA Modules:
  0.0 235.2 jit_solution(4597328169797305027)
XLA Ops:
  6.5 0.0 copy-start.6
  6.5 0.0 copy-start.1
  6.5 0.0 copy-start.2
  6.5 0.0 copy-start.3
  6.5 0.0 copy-start.4
  6.5 0.0 copy-start.5
  6.6 0.0 all-gather.2.cloned.1.call-start
  6.6 1.5 collective-permute-start
  8.1 4.0 %collective-permute-done = bf16[16,64,1024]{2,1,0:T(8,128)(2,1)S(1)} collective-permute-done((bf16[16,64,1024]{2,1,0:T(8,128)(2,1)}, bf16[16,64,1024]{2,1,0:T(8,128)(2,1)S(1)}, u32[]{:S(2)}, u32[]{:S(2)}) %collective-permute-start) | collective-permute-done | bytes 2097184 | tf_op jit(solution)/shard_map/ppermute | solution.py:11
  12.1 0.0 copy-start
  12.1 1.3 copy-done
  13.4 0.0 all-gather.2.cloned.1.call-update
  14.1 2.7 %copy.11 = bf16[2,8,64,1024]{3,1,2,0:T(8,128)(2,1)S(1)} copy(bf16[2,8,64,1024]{3,2,1,0:T(8,128)(2,1)} %bitcast.49) | data formatting | bytes 4194304
  16.8 0.0 copy-done.6
  16.9 0.6 dynamic-slice
  18.1 0.7 bitcast_dynamic-update-slice_fusion.2
  18.8 0.0 copy-done.1
  18.8 0.1 bitcast_dynamic-update-slice_fusion.4
  18.9 0.0 copy-done.2
  18.9 0.1 bitcast_dynamic-update-slice_fusion.1
  19.0 0.0 copy-done.3
  19.0 0.1 bitcast_dynamic-update-slice_fusion.3
  19.1 0.0 copy-done.4
  19.1 0.1 bitcast_dynamic-update-slice_fusion
  19.2 13.6 %all-reduce.5 = (s32[48]{0:T(128)S(1)}, s32[48]{0:T(128)S(1)}, s32[16]{0:T(128)S(1)}, s32[48]{0:T(128)S(1)}, s32[48]{0:T(128)S(1)}) all-reduce(s32[48]{0:T(128)S(1)} %bitcast_dynamic-update-slice_fusion.3, s32[48]{0:T(128)S(1)} %bitcast_dynamic-update-slice_fusion.1, ...), channel_id=1, replica_groups=mesh['mom'=8,'pair'=16] {'pair'}, use_global_device_ids=true, to_apply=%add.1 | all-reduce | flops 208 | bytes 1664
  32.9 0.0 copy-done.5
  32.9 0.1 select_reduce_fusion.1
  32.9 0.1 select_reduce_fusion
  33.1 0.1 fusion.8
  33.2 3.6 %convolution_convert_fusion = bf16[32,65536]{1,0:T(8,128)(2,1)S(1)} fusion(f32[32,16]{1,0:T(8,128)S(1)} %bitcast.50, bf16[16,65536]{1,0:T(8,128)(2,1)S(1)} %bitcast.47), kind=kOutput, calls=%fused_computation | convolution fusion | flops 404750336 | bytes 6293504 | tf_op jit(solution)/shard_map/dot_general | solution.py:36
  36.8 4.4 %copy.12 = bf16[4,8,64,1024]{3,2,1,0:T(8,128)(2,1)} copy(bf16[4,8,64,1024]{3,1,2,0:T(8,128)(2,1)S(1)} %bitcast.46) | data formatting | bytes 8388608
  41.1 171.9 %all-gather.2.cloned.1.call-done = bf16[16,1024,1024]{2,1,0:T(8,128)(2,1)} async-done(((bf16[16,64,1024]{2,1,0:T(8,128)(2,1)}), bf16[16,1024,1024]{2,1,0:T(8,128)(2,1)}) %all-gather.2.cloned.1.call-update) | async-done | bytes 33554448 | tf_op jit(solution)/shard_map/all_gather | solution.py:66
  213.0 14.1 %fusion.3 = f32[1,64,2,1024]{3,1,2,0:T(8,128)S(1)} fusion(bf16[16,1024,1024]{2,1,0:T(8,128)(2,1)} %all-gather.2.cloned.1.call-done, bf16[2,16,64,1024]{3,2,1,0:T(8,128)(2,1)} %bitcast.45), kind=kOutput, calls=%fused_computation.4 | convolution fusion | flops 4294967296 | bytes 38273024 | tf_op jit(solution)/shard_map/tbij,bjl->itl/dot_general | solution.py:63
  227.1 1.2 copy.9
  (9 shorter events, 0.0 us)
Async XLA Ops:
  6.5 10.3 %copy-start.6 = (u32[128]{0:T(128)S(1)}, u32[128]{0:T(128)}, u32[]{:S(2)}) copy-start(u32[128]{0:T(128)} %constant.32) | copy-start | bytes 1540
  6.5 12.3 %copy-start.1 = (s32[1,3]{1,0:T(1,128)S(1)}, s32[1,3]{1,0:T(1,128)}, u32[]{:S(2)}) copy-start(s32[1,3]{1,0:T(1,128)} %param.9) | copy-start | bytes 40
  6.5 12.4 %copy-start.2 = (s32[1,3]{1,0:T(1,128)S(1)}, s32[1,3]{1,0:T(1,128)}, u32[]{:S(2)}) copy-start(s32[1,3]{1,0:T(1,128)} %param.11) | copy-start | bytes 40
  6.5 12.5 %copy-start.3 = (s32[1,3]{1,0:T(1,128)S(1)}, s32[1,3]{1,0:T(1,128)}, u32[]{:S(2)}) copy-start(s32[1,3]{1,0:T(1,128)} %param.10) | copy-start | bytes 40
  6.5 12.6 %copy-start.4 = (s32[1,3]{1,0:T(1,128)S(1)}, s32[1,3]{1,0:T(1,128)}, u32[]{:S(2)}) copy-start(s32[1,3]{1,0:T(1,128)} %param.8) | copy-start | bytes 40
  6.5 26.3 %copy-start.5 = (f32[8]{0:T(128)S(1)}, f32[8]{0:T(128)}, u32[]{:S(2)}) copy-start(f32[8]{0:T(128)} %param.13) | copy-start | bytes 100
  6.6 206.5 %all-gather.2.cloned.1.call-start = ((), (), s32[]{:S(2)}) async-start(), calls=%async_computation | async-start | bytes 35651584 | tf_op jit(solution)/shard_map/all_gather | solution.py:66
  6.6 5.5 %collective-permute-start = (bf16[16,64,1024]{2,1,0:T(8,128)(2,1)}, bf16[16,64,1024]{2,1,0:T(8,128)(2,1)S(1)}, u32[]{:S(2)}, u32[]{:S(2)}) collective-permute-start(bf16[16,64,1024]{2,1,0:T(8,128)(2,1)} %bitcast.48), channel_id=1, source_target_pairs={{0,16},{16,0},{32,48},{48,32},{64,80},{80,64},{96,112},{112,96},{1... | collective-permute-start | bytes 6291464 | tf_op jit(solution)/shard_map/ppermute | solution.py:11
  12.1 1.3 copy-start
Sparse Core Ops, SparseCore 0:
  13.6 199.4 all-gather.1
where the time goes:
time: 235 us
  waiting for transfers between devices  176 us (75%)
  matrix products  17.8 us (8%)
  between operations  14.8 us (6%)
  blocking collectives  13.6 us (6%)
  local copies, waits for them, and re-layouts  11.3 us (5%)
    all_gather x1, waiting for transfers between devices, body(): lax.all_gather(partner, 'pair', axis=1, tiled=True)  172 us
    dot_general x1, matrix products, body(): jnp.einsum('tbij,bjl->itl', combined, lax.all_gather(partner, 'pair', axi...  14.1 us
    unnamed x1, blocking collectives  13.6 us
    unnamed x27, local copies, waits for them, and re-layouts  10.1 us
  transfers between devices with their start and end apart: 2, of which 2 were waited for; matrix products, arithmetic and copies ran while one was open for 5% of the time, Pallas kernels for 0%

commit v1 on v0

--- a/solution.py
+++ b/solution.py
@@ -63,7 +63,9 @@
     result = jnp.einsum(
         "tbij,bjl->itl",
         combined,
-        lax.all_gather(partner, "pair", axis=1, tiled=True),
+        jnp.concatenate(
+            lax.all_to_all(jnp.stack([partner] * lax.axis_size("pair")), "pair", 0, 0), axis=1
+        ),
         preferred_element_type=jnp.float32,
     )
     return result.reshape((1,) + result.shape)

time: 235 us -> 699 us (2.97)
  blocking collectives: 13.6 us -> 617 us
  waiting for transfers between devices: 176 us -> 4 us
  local copies, waits for them, and re-layouts: 11.3 us -> 44 us
  between operations: 14.8 us -> 1.48 us
  starting transfers between devices: 1.54 us -> 9.15 us
    unnamed x1, blocking collectives: 13.6 us -> 617 us
    all_gather x1 -> x0, waiting for transfers between devices: 172 us -> none  [body(): lax.all_gather(partner, 'pair', axis=1, tiled=True)]
    reshape x0 -> x1, local copies, waits for them, and re-layouts: none -> 23.1 us  [body(): jnp.concatenate(lax.all_to_all(jnp.stack([partner] * lax.axis_size('pair'...]
    another operation x0 -> x1, local copies, waits for them, and re-layouts: none -> 11 us  [body(): jnp.stack([partner] * lax.axis_size('pair'))]
    all_to_all x0 -> x1, starting transfers between devices: none -> 7.73 us  [body(): lax.all_to_all(jnp.stack([partner] * lax.axis_size('pair')), 'pair', 0, 0)]
  transfers between devices with their start and end apart: 2 -> 2, of which waited for: 2 -> 1; matrix products, arithmetic and copies ran while one was open for 5% -> 2% of each run, Pallas kernels for 0% -> 0%
where the time goes in v1:
time: 699 us; the launch traced here: 693 us
  blocking collectives  617 us (88%)
  local copies, waits for them, and re-layouts  44 us (6%)
  matrix products  17.8 us (3%)
  starting transfers between devices  9.15 us (1%)
    unnamed x1, blocking collectives  617 us
    reshape x1, local copies, waits for them, and re-layouts, body(): jnp.concatenate(lax.all_to_all(jnp.stack([partner] * lax.axis_size('pair'...  23.1 us
    dot_general x1, matrix products, body(): jnp.einsum('tbij,bjl->itl', combined, jnp.concatenate(lax.all_to_all(jnp....  14.1 us
  transfers between devices with their start and end apart: 2, of which 1 were waited for; matrix products, arithmetic and copies ran while one was open for 2% of the time, Pallas kernels for 0%

profile of v1, /device:TPU:1, one launch (start us, length us, event | category | flops | bytes accessed | tf_op | source)
XLA Modules:
  0.0 693.4 jit_solution(12767800785091776527)
XLA Ops:
  0.0 1.4 collective-permute-start
  1.4 4.0 collective-permute-done
  5.4 11.0 %stack.2 = bf16[16,16,64,1024]{3,2,1,0:T(8,128)(2,1)} broadcast(bf16[16,64,1024]{2,1,0:T(8,128)(2,1)S(1)} %collective-permute-done), dimensions={1,2,3} | broadcast | bytes 35651584 | tf_op jit(solution)/shard_map/stack | solution.py:67
  16.4 7.7 %all-to-all-start = ((bf16[16,16,64,1024]{3,2,1,0:T(8,128)(2,1)}), bf16[16,16,64,1024]{3,2,1,0:T(8,128)(2,1)}, u32[]{:S(2)}, u32[]{:S(2)}) async-start(bf16[16,16,64,1024]{3,2,1,0:T(8,128)(2,1)} %stack.2), calls=%async_computation | async-start | bytes 67108864 | tf_op jit(solution)/shard_map/all_to_all | solution.py:67
  24.2 0.0 copy-start.5
  24.2 0.0 copy-start
  24.2 0.0 copy-start.1
  24.2 0.0 copy-start.2
  24.2 0.0 copy-start.3
  24.2 0.0 copy-start.4
  24.9 2.7 copy.14
  27.7 0.0 copy-done.5
  27.7 0.6 dynamic-slice
  28.9 0.7 bitcast_dynamic-update-slice_fusion.2
  29.6 0.0 copy-done
  29.6 0.1 bitcast_dynamic-update-slice_fusion.3
  29.7 0.0 copy-done.1
  29.7 0.1 bitcast_dynamic-update-slice_fusion.1
  29.8 0.0 copy-done.2
  29.8 0.1 bitcast_dynamic-update-slice_fusion.4
  29.9 0.0 copy-done.3
  29.9 0.1 bitcast_dynamic-update-slice_fusion
  30.0 616.7 %all-reduce.5 = (s32[48]{0:T(128)S(1)}, s32[48]{0:T(128)S(1)}, s32[16]{0:T(128)S(1)}, s32[48]{0:T(128)S(1)}, s32[48]{0:T(128)S(1)}) all-reduce(s32[48]{0:T(128)S(1)} %bitcast_dynamic-update-slice_fusion.3, s32[48]{0:T(128)S(1)} %bitcast_dynamic-update-slice_fusion.1, ...), channel_id=1, replica_groups=mesh['mom'=8,'pair'=16] {'pair'}, use_global_device_ids=true, to_apply=%add.1 | all-reduce | flops 208 | bytes 1664
  646.8 0.0 copy-done.4
  646.8 0.1 select_reduce_fusion.1
  646.9 0.1 select_reduce_fusion
  647.0 0.1 fusion.5
  647.1 3.6 convolution_convert_fusion
  650.7 4.3 copy.15
  655.0 0.0 all-to-all-done
  655.0 23.1 %copy.11 = bf16[16,16,64,1024]{3,2,1,0:T(8,128)(2,1)} copy(bf16[16,16,64,1024]{3,2,0,1:T(8,128)(2,1)} %bitcast.11) | data formatting | bytes 67108864 | tf_op jit(solution)/shard_map/reshape | solution.py:66
  678.1 14.1 %fusion.2 = f32[1,64,2,1024]{3,1,2,0:T(8,128)S(1)} fusion(bf16[16,1024,1024,1]{2,1,0,3:T(8,128)(2,1)} %bitcast.45, bf16[2,16,64,1024]{3,2,1,0:T(8,128)(2,1)} %bitcast.46), kind=kOutput, calls=%fused_computation.3 | convolution fusion | flops 4294967296 | bytes 38273024 | tf_op jit(solution)/shard_map/tbij,bjl->itl/dot_general | solution.py:63
  692.2 1.2 copy.12
  (9 shorter events, 0.0 us)
Async XLA Ops:
  0.0 5.4 collective-permute-start
  16.4 638.6 %all-to-all-start = ((bf16[16,16,64,1024]{3,2,1,0:T(8,128)(2,1)}), bf16[16,16,64,1024]{3,2,1,0:T(8,128)(2,1)}, u32[]{:S(2)}, u32[]{:S(2)}) async-start(bf16[16,16,64,1024]{3,2,1,0:T(8,128)(2,1)} %stack.2), calls=%async_computation | async-start | bytes 67108864 | tf_op jit(solution)/shard_map/all_to_all | solution.py:67
  24.2 3.5 copy-start.5
  24.2 5.4 copy-start
  24.2 5.5 copy-start.1
  24.2 5.6 copy-start.2
  24.2 5.7 copy-start.3
  24.2 622.5 %copy-start.4 = (f32[8]{0:T(128)S(1)}, f32[8]{0:T(128)}, u32[]{:S(2)}) copy-start(f32[8]{0:T(128)} %param.13) | copy-start | bytes 100
